TPU v7x, 512 devices: a whole 4x4x16 slice. The times are simulated.
512 devices in a mesh: row: 32 (over x, y, core), col: 16 (over z).
Axes of the slice: x: 4, y: 4, z: 16, core: 2. Of those that a mesh axis runs over, the one named last changes fastest.
Arguments:
- descriptors: bfloat16 [32, 98304], P(None, ('row', 'col')), may hold values from -6 to 6
- densities: float32 [98304], P(('row', 'col')), may hold values from 0.25 to 4
- vectors: float32 [32, 98304], P(None, ('row', 'col')), may hold values from -6 to 6
Outputs:
- next_block: float32 [32, 98304], P(None, ('row', 'col'))
All inputs are finite; a program needn't handle non-finite values.
Results may differ from a plain program's by a relative error of at most 0.0036.
Values may be sent and summed in bfloat16 or wider, within the bound.
A program may use at most 64 MiB of HBM per device.

v0:
```python
import math
import jax
import jax.numpy as jnp
from jax import lax
from jax.sharding import Mesh
from jax.sharding import PartitionSpec as P

ROW = ("row_0", "row_1", "row_2")
ROW_COL = ("row_0", "row_1", "row_2", "col")
kernel_width = 8.0


def from_everyone(shard, axis):
    count = lax.axis_size(axis)
    return lax.all_to_all(
        jnp.broadcast_to(shard[None], (count, *shard.shape)), axis, 0, 0, tiled=True
    )


def laid_out(tiles, dim):
    shape = list(tiles.shape[1:])
    shape[dim] *= tiles.shape[0]
    return jnp.moveaxis(tiles, 0, dim).reshape(shape)


def gather_directly(shard, axis, dim):
    tiles = from_everyone(shard, axis)
    return laid_out(tiles, dim)


def turned_gather(arrays, axis, dims):
    turned = [jnp.moveaxis(a, dim, 0) for a, dim in zip(arrays, dims)]
    widths = [t[0].size for t in turned]
    both = jnp.concatenate([t.reshape(-1, w) for t, w in zip(turned, widths)], axis=1)
    filled = lax.all_gather(both, axis, axis=0, tiled=True)
    tiles = jnp.split(filled, [sum(widths[:k]) for k in range(1, len(widths))], axis=1)
    return tuple(
        (
            jnp.moveaxis(b.reshape(-1, *t.shape[1:]), 0, dim)
            for b, t, dim in zip(tiles, turned, dims)
        )
    )


def cut_along(shard, dim, count):
    before, after = (shard.shape[:dim], shard.shape[dim + 1 :])
    return jnp.moveaxis(shard.reshape(*before, count, -1, *after), dim, 0)


def sent_and_summed(shard, axis, dim):
    count = lax.axis_size(axis)
    tiles = lax.all_to_all(cut_along(shard, dim, count), axis, 0, 0, tiled=True)
    return jnp.sum(tiles, axis=0)


def side_by_side(arrays, axis, dim, along):
    ends, at = ([], 0)
    for a in arrays[:-1]:
        at += a.shape[along]
        ends.append(at)
    both = jnp.concatenate(arrays, axis=along)
    return tuple(jnp.split(sent_and_summed(both, axis, dim), ends, axis=along))


def over_copies(shard, axis):
    return from_everyone(shard, axis).sum(axis=0)


def one_axis_at_a_time(shard, axes):
    far, near = axes
    return over_copies(over_copies(shard, near), far)


def in_one(arrays, axis):
    flat, at, finished = (jnp.concatenate([a.reshape(-1) for a in arrays]), 0, [])
    running = one_axis_at_a_time(flat, axis)
    for a in arrays:
        finished.append(running[at : at + a.size].reshape(a.shape))
        at += a.size
    return tuple(finished)


def tile_terms(targets, target_norm, piece):
    piece_feat, piece_vals, piece_inv = piece
    piece_norm = jnp.sum(jnp.square(piece_feat.astype(jnp.float32)), axis=0)
    feature_dim, target_count = targets.shape
    span_rows = math.gcd(target_count, 512)
    block_count = target_count // span_rows
    blocks = targets.reshape(feature_dim, block_count, span_rows).transpose(1, 0, 2)
    norm_blocks = target_norm.reshape(block_count, span_rows)

    def tile_block(block_item):
        block_feat, block_norm = block_item
        inner_prod = lax.dot_general(
            block_feat, piece_feat, (((0,), (0,)), ((), ())), preferred_element_type=jnp.float32
        )
        kernel = jnp.exp(
            -(block_norm[:, None] + piece_norm[None, :] - 2.0 * inner_prod) / kernel_width
        ).astype(jnp.bfloat16)
        numerator = lax.dot_general(
            piece_vals, kernel, (((1,), (1,)), ((), ())), preferred_element_type=jnp.float32
        )
        degree = lax.dot_general(
            piece_inv, kernel, (((1,), (1,)), ((), ())), preferred_element_type=jnp.float32
        )
        return (numerator, degree)

    numerator, degree = lax.map(tile_block, (blocks, norm_blocks))
    numerator = numerator.transpose(1, 0, 2).reshape(piece_vals.shape[0], target_count)
    degree = degree.transpose(1, 0, 2).reshape(1, target_count)
    return (numerator, degree)


def accumulate(targets, vec_count):
    target_norm = jnp.sum(jnp.square(targets.astype(jnp.float32)), axis=0)

    def fold_piece(running, piece, start):
        numerator, degree = tile_terms(targets, target_norm, piece)
        return (numerator, degree)

    initial = (
        jnp.zeros((vec_count, targets.shape[1]), jnp.float32),
        jnp.zeros((1, targets.shape[1]), jnp.float32),
    )
    return (fold_piece, initial)


def per_device(descriptors, densities, vectors):
    highest = lax.Precision.HIGHEST
    vec_count = vectors.shape[0]
    weighted = (vectors / densities[None, :]).astype(jnp.bfloat16)
    inverse = (1.0 / densities).astype(jnp.bfloat16)[None, :]
    targets = gather_directly(descriptors, ROW, 1)
    fold_piece, initial = accumulate(targets, vec_count)
    partial_value = fold_piece(
        initial, turned_gather((descriptors, weighted, inverse), "col", (1, 1, 1)), jnp.int32(0)
    )
    numerator, degree = side_by_side((partial_value[0], partial_value[1]), ROW, 1, 0)
    diffused = numerator / degree
    samples_float = float(descriptors.shape[1] * lax.axis_size(ROW) * lax.axis_size("col"))
    coupling, diffused_gram, basis_gram = in_one(
        (
            jnp.dot(vectors, diffused.T, precision=highest),
            jnp.dot(diffused, diffused.T, precision=highest),
            jnp.dot(vectors, vectors.T, precision=highest),
        ),
        (("row_0", "row_1"), ("row_2", "col")),
    )
    remainder = diffused - jnp.dot(coupling.T, vectors, precision=highest) / samples_float
    cross_term = jnp.dot(coupling.T, coupling, precision=highest)
    basis_term = jnp.dot(
        coupling.T, jnp.dot(basis_gram, coupling, precision=highest), precision=highest
    )
    spread = (
        diffused_gram
        - 2.0 * cross_term / samples_float
        + basis_term / (samples_float * samples_float)
    )
    factor = jnp.linalg.cholesky(spread)
    solved = jax.scipy.linalg.solve_triangular(factor, remainder, lower=True)
    return math.sqrt(samples_float) * solved


def solution(mesh):
    finer = Mesh(
        mesh.devices.reshape(4, 4, 2, mesh.shape["col"]), ("row_0", "row_1", "row_2", "col")
    )
    placed = (P(None, ROW_COL), P(ROW_COL), P(None, ROW_COL))
    return jax.shard_map(
        per_device, mesh=finer, in_specs=placed, out_specs=P(None, ROW_COL), check_vma=False
    )
```

profile of v0, /device:TPU:1, one launch (start us, length us, event | category | flops | bytes accessed | tf_op | source)
XLA Modules:
  0.0 182.3 jit_solution(6465203450939220424)
XLA Ops:
  0.0 1.6 broadcast_in_dim.23
  1.6 10.4 %all-to-all-start = ((bf16[32,32,192]{2,1,0:T(8,128)(2,1)}), bf16[32,32,192]{2,1,0:T(8,128)(2,1)S(1)}, u32[]{:S(2)}, u32[]{:S(2)}) async-start(bf16[32,32,192]{2,1,0:T(8,128)(2,1)} %broadcast_in_dim.23), calls=%async_computation | async-start | bytes 1048576 | tf_op jit(solution)/shard_map/all_to_all | solution.py:15
  14.2 29.9 %all-gather = bf16[16,192,65]{1,2,0:T(8,128)(2,1)S(1)} all-gather(bf16[1,192,65]{1,2,0:T(8,128)(2,1)S(1)} %maximum_bitcast_fusion.1), channel_id=1, replica_groups=mesh['row_0'=4,'row_1'=4,'row_2'=2,'col'=16] {'col'}, dimensions={0}, use_global_device_ids=true | all-gather | bytes 424320 | tf_op jit(solution)/shard_map/all_gather | solution.py:35
  46.5 43.8 %while.12 = (s32[]{:T(128)}, f32[12,32,512]{2,1,0:T(8,128)S(1)}, f32[12,1,512]{2,1,0:T(1,128)S(1)}, f32[12,512]{1,0:T(8,128)S(1)}, f32[3072]{0:T(1024)S(1)}, /*i...) while((s32[]{:T(128)}, f32[12,32,512]{2,1,0:T(8,128)S(1)}, ...), condition=%wide.region_3.4_spmd, body=%wide.region_2.3_spmd.sunk | while | flops 213909504 | bytes 9961589 | solution.py:108
  46.5 1.7 exponential_convert_fusion.2
  50.1 1.7 exponential_convert_fusion.2
  51.8 1.0 fusion.47
  53.8 1.7 exponential_convert_fusion.2
  57.5 1.7 exponential_convert_fusion.2
  61.1 1.7 exponential_convert_fusion.2
  64.8 1.7 exponential_convert_fusion.2
  68.4 1.7 exponential_convert_fusion.2
  72.1 1.7 exponential_convert_fusion.2
  75.7 1.7 exponential_convert_fusion.2
  79.4 1.7 exponential_convert_fusion.2
  83.0 1.7 exponential_convert_fusion.2
  86.7 1.7 exponential_convert_fusion.2
  91.6 1.7 copy.49
  93.3 14.3 %all-to-all-start.1 = ((f32[32,33,192]{2,1,0:T(8,128)}), f32[32,33,192]{2,1,0:T(8,128)S(1)}, u32[]{:S(2)}, u32[]{:S(2)}) async-start(f32[32,33,192]{2,1,0:T(8,128)} %copy.49), calls=%async_computation.1 | async-start | bytes 2621440 | tf_op jit(solution)/shard_map/all_to_all | solution.py:52
  107.9 19.5 %all-to-all-done.1 = f32[32,33,192]{2,1,0:T(8,128)S(1)} async-done(((f32[32,33,192]{2,1,0:T(8,128)}), f32[32,33,192]{2,1,0:T(8,128)S(1)}, u32[]{:S(2)}, u32[]{:S(2)}) %all-to-all-start.1) | async-done | bytes 811040 | tf_op jit(solution)/shard_map/all_to_all | solution.py:52
  128.3 33.9 %all_to_all.22 = f32[32,1,3072]{2,1,0:T(1,128)S(1)} all-to-all(f32[32,1,3072]{2,1,0:T(1,128)S(1)} %broadcast_in_dim.40), channel_id=1, replica_groups=mesh['row_0'=4,'row_1'=4,'row_2'=2,'col'=16] {'row_2','col'}, dimensions={0} | all-to-all | bytes 786432 | tf_op jit(solution)/shard_map/all_to_all | solution.py:15
  162.5 10.9 %all_to_all.23 = f32[16,1,3072]{2,1,0:T(1,128)S(1)} all-to-all(f32[16,1,3072]{2,1,0:T(1,128)S(1)} %broadcast_in_dim.41), channel_id=1, replica_groups=mesh['row_0'=4,'row_1'=4,'row_2'=2,'col'=16] {'row_0','row_1'}, dimensions={0} | all-to-all | bytes 393216 | tf_op jit(solution)/shard_map/all_to_all | solution.py:15
  174.8 2.9 %cholesky.16 = f32[32,32]{1,0:T(8,128)S(1)} custom-call(f32[32,32]{1,0:T(8,128)S(1)} %fusion.11), custom_call_target="Cholesky" | custom-call | tf_op jit(solution)/shard_map/jit(cholesky)/cholesky | solution.py:159
  179.0 2.4 %custom-call.7 = f32[1,32,32]{1,2,0:T(8,128)S(1)} custom-call(f32[1,32,32]{2,1,0:T(8,128)S(1)} %fusion.9), custom_call_target="InvertDiagBlocksLowerTriangular" | custom-call | tf_op jit(solution)/shard_map/jit(_solve_triangular)/triangular_solve | solution.py:160
  (88 shorter events, 33.4 us)
Async XLA Ops:
  1.6 43.4 %all-to-all-start = ((bf16[32,32,192]{2,1,0:T(8,128)(2,1)}), bf16[32,32,192]{2,1,0:T(8,128)(2,1)S(1)}, u32[]{:S(2)}, u32[]{:S(2)}) async-start(bf16[32,32,192]{2,1,0:T(8,128)(2,1)} %broadcast_in_dim.23), calls=%async_computation | async-start | bytes 1048576 | tf_op jit(solution)/shard_map/all_to_all | solution.py:15
  91.5 16.1 %copy-start = (f32[32,192]{1,0:T(8,128)S(1)}, f32[32,192]{1,0:T(8,128)}, u32[]{:S(2)}) copy-start(f32[32,192]{1,0:T(8,128)} %param.7) | copy-start | bytes 73732
  93.3 34.1 %all-to-all-start.1 = ((f32[32,33,192]{2,1,0:T(8,128)}), f32[32,33,192]{2,1,0:T(8,128)S(1)}, u32[]{:S(2)}, u32[]{:S(2)}) async-start(f32[32,33,192]{2,1,0:T(8,128)} %copy.49), calls=%async_computation.1 | async-start | bytes 2621440 | tf_op jit(solution)/shard_map/all_to_all | solution.py:52
where the time goes:
time: 183 us; the launch traced here: 182 us
  blocking collectives  74.7 us (41%)
  matrix products  45.7 us (25%)
  starting transfers between devices  24.7 us (13%)
  waiting for transfers between devices  19.5 us (11%)
  other arithmetic  9.74 us (5%)
  local copies, waits for them, and re-layouts  7.53 us (4%)
    all_to_all x2, blocking collectives, from_everyone(): lax.all_to_all(jnp.broadcast_to(shard[None], (count, *shard.shape)), axis...  44.8 us
    all_gather x1, blocking collectives, turned_gather(): filled = lax.all_gather(both, axis, axis=0, tiled=True)  29.9 us
    dot_general x12, matrix products, tile_block(): lax.dot_general(block_feat, piece_feat, (((0,), (0,)), ((), ())), preferr...  19.9 us
    all_to_all x1, waiting for transfers between devices, sent_and_summed(): tiles = lax.all_to_all(cut_along(shard, dim, count), axis, 0, 0, tiled=True)  19.5 us
    all_to_all x1, starting transfers between devices, sent_and_summed(): tiles = lax.all_to_all(cut_along(shard, dim, count), axis, 0, 0, tiled=True)  14.3 us
    dot_general x12, matrix products, tile_block(): lax.dot_general(piece_vals, kernel, (((1,), (1,)), ((), ())), preferred_e...  12.5 us
    dot_general x12, matrix products, tile_block(): lax.dot_general(piece_inv, kernel, (((1,), (1,)), ((), ())), preferred_el...  11.2 us
    all_to_all x1, starting transfers between devices, from_everyone(): lax.all_to_all(jnp.broadcast_to(shard[None], (count, *shard.shape)), axis...  10.4 us
  transfers between devices with their start and end apart: 2, of which 1 were waited for; matrix products, arithmetic and copies ran while one was open for 2% of the time, Pallas kernels for 0%

commit v1 on v0

--- a/solution.py
+++ b/solution.py
@@ -32,7 +32,9 @@
     turned = [jnp.moveaxis(a, dim, 0) for a, dim in zip(arrays, dims)]
     widths = [t[0].size for t in turned]
     both = jnp.concatenate([t.reshape(-1, w) for t, w in zip(turned, widths)], axis=1)
-    filled = lax.all_gather(both, axis, axis=0, tiled=True)
+    filled = jnp.concatenate(
+        lax.all_to_all(jnp.stack([both] * lax.axis_size(axis)), axis, 0, 0), axis=0
+    )
     tiles = jnp.split(filled, [sum(widths[:k]) for k in range(1, len(widths))], axis=1)
     return tuple(
         (

time: 183 us -> 196 us (1.071)
  waiting for transfers between devices: 19.5 us -> 55.7 us
  blocking collectives: 74.7 us -> 43.8 us
  starting transfers between devices: 24.7 us -> 31.9 us
    all_gather x1 -> x0, blocking collectives: 29.9 us -> none  [turned_gather(): filled = lax.all_gather(both, axis, axis=0, tiled=True)]
    all_to_all x0 -> x1, waiting for transfers between devices: none -> 26.6 us  [turned_gather(): lax.all_to_all(jnp.stack([both] * lax.axis_size(axis)), axis, 0, 0)]
    all_to_all x0 -> x1, starting transfers between devices: none -> 13 us  [turned_gather(): lax.all_to_all(jnp.stack([both] * lax.axis_size(axis)), axis, 0, 0)]
    all_to_all x1, waiting for transfers between devices: 0.01 us -> 9.54 us  [from_everyone(): lax.all_to_all(jnp.broadcast_to(shard[None], (count, *shard.shape)), axis...]
    all_to_all x1, starting transfers between devices: 14.3 us -> 8.53 us  [sent_and_summed(): tiles = lax.all_to_all(cut_along(shard, dim, count), axis, 0, 0, tiled=True)]
  transfers between devices with their start and end apart: 2 -> 3, of which waited for: 1 -> 3; matrix products, arithmetic and copies ran while one was open for 2% -> 2% of each run, Pallas kernels for 0% -> 0%
where the time goes in v1:
time: 196 us
  waiting for transfers between devices  55.7 us (28%)
  matrix products  45.7 us (23%)
  blocking collectives  43.8 us (22%)
  starting transfers between devices  31.9 us (16%)
  other arithmetic  9.74 us (5%)
  local copies, waits for them, and re-layouts  8.38 us (4%)
    all_to_all x2, blocking collectives, from_everyone(): lax.all_to_all(jnp.broadcast_to(shard[None], (count, *shard.shape)), axis...  43.8 us
    all_to_all x1, waiting for transfers between devices, turned_gather(): lax.all_to_all(jnp.stack([both] * lax.axis_size(axis)), axis, 0, 0)  26.6 us
    dot_general x12, matrix products, tile_block(): lax.dot_general(block_feat, piece_feat, (((0,), (0,)), ((), ())), preferr...  19.9 us
    all_to_all x1, waiting for transfers between devices, sent_and_summed(): tiles = lax.all_to_all(cut_along(shard, dim, count), axis, 0, 0, tiled=True)  19.6 us
    all_to_all x1, starting transfers between devices, turned_gather(): lax.all_to_all(jnp.stack([both] * lax.axis_size(axis)), axis, 0, 0)  13 us
    dot_general x12, matrix products, tile_block(): lax.dot_general(piece_vals, kernel, (((1,), (1,)), ((), ())), preferred_e...  12.5 us
    dot_general x12, matrix products, tile_block(): lax.dot_general(piece_inv, kernel, (((1,), (1,)), ((), ())), preferred_el...  11.2 us
    all_to_all x1, starting transfers between devices, from_everyone(): lax.all_to_all(jnp.broadcast_to(shard[None], (count, *shard.shape)), axis...  10.4 us
  transfers between devices with their start and end apart: 3, of which 3 were waited for; matrix products, arithmetic and copies ran while one was open for 2% of the time, Pallas kernels for 0%

profile of v1, /device:TPU:1, one launch (start us, length us, event | category | flops | bytes accessed | tf_op | source)
XLA Modules:
  0.0 195.7 jit_solution(6593952178241605016)
XLA Ops:
  1.6 10.4 %all-to-all-start = ((bf16[32,32,192]{2,1,0:T(8,128)(2,1)}), bf16[32,32,192]{2,1,0:T(8,128)(2,1)S(1)}, u32[]{:S(2)}, u32[]{:S(2)}) async-start(bf16[32,32,192]{2,1,0:T(8,128)(2,1)} %broadcast_in_dim.23), calls=%async_computation | async-start | bytes 1048576 | tf_op jit(solution)/shard_map/all_to_all | solution.py:15
  14.2 9.5 %all-to-all-done = bf16[32,32,192]{2,1,0:T(8,128)(2,1)S(1)} async-done(((bf16[32,32,192]{2,1,0:T(8,128)(2,1)}), bf16[32,32,192]{2,1,0:T(8,128)(2,1)S(1)}, u32[]{:S(2)}, u32[]{:S(2)}) %all-to-all-start) | async-done | bytes 393248 | tf_op jit(solution)/shard_map/all_to_all | solution.py:15
  24.6 13.0 %all-to-all-start.1 = ((bf16[16,192,65]{1,2,0:T(8,128)(2,1)}), bf16[16,192,65]{1,2,0:T(8,128)(2,1)S(1)}, u32[]{:S(2)}, u32[]{:S(2)}) async-start(bf16[16,192,65]{1,2,0:T(8,128)(2,1)} %stack.2), calls=%async_computation.1 | async-start | bytes 1179648 | tf_op jit(solution)/shard_map/all_to_all | solution.py:36
  39.1 26.6 %all-to-all-done.1 = bf16[16,192,65]{1,2,0:T(8,128)(2,1)S(1)} async-done(((bf16[16,192,65]{1,2,0:T(8,128)(2,1)}), bf16[16,192,65]{1,2,0:T(8,128)(2,1)S(1)}, u32[]{:S(2)}, u32[]{:S(2)}) %all-to-all-start.1) | async-done | bytes 399392 | tf_op jit(solution)/shard_map/all_to_all | solution.py:36
  66.6 43.9 %while.12 = (s32[]{:T(128)}, f32[12,32,512]{2,1,0:T(8,128)S(1)}, f32[12,1,512]{2,1,0:T(1,128)S(1)}, f32[12,512]{1,0:T(8,128)S(1)}, f32[3072]{0:T(1024)S(1)}, /*i...) while((s32[]{:T(128)}, f32[12,32,512]{2,1,0:T(8,128)S(1)}, ...), condition=%wide.region_3.4_spmd, body=%wide.region_2.3_spmd.sunk | while | flops 213909504 | bytes 9961589 | solution.py:110
  66.6 1.7 exponential_convert_fusion.2
  70.2 1.7 exponential_convert_fusion.2
  73.9 1.7 exponential_convert_fusion.2
  77.5 1.7 exponential_convert_fusion.2
  81.2 1.7 exponential_convert_fusion.2
  84.9 1.7 exponential_convert_fusion.2
  88.5 1.7 exponential_convert_fusion.2
  92.2 1.7 exponential_convert_fusion.2
  95.8 1.7 exponential_convert_fusion.2
  99.5 1.7 exponential_convert_fusion.2
  103.1 1.7 exponential_convert_fusion.2
  106.8 1.7 exponential_convert_fusion.2
  111.7 1.7 copy.47
  113.4 8.5 %all-to-all-start.2 = ((f32[32,33,192]{2,1,0:T(8,128)}), f32[32,33,192]{2,1,0:T(8,128)S(1)}, u32[]{:S(2)}, u32[]{:S(2)}) async-start(f32[32,33,192]{2,1,0:T(8,128)} %copy.47), calls=%async_computation.2 | async-start | bytes 2621440 | tf_op jit(solution)/shard_map/all_to_all | solution.py:54
  122.2 19.6 %all-to-all-done.2 = f32[32,33,192]{2,1,0:T(8,128)S(1)} async-done(((f32[32,33,192]{2,1,0:T(8,128)}), f32[32,33,192]{2,1,0:T(8,128)S(1)}, u32[]{:S(2)}, u32[]{:S(2)}) %all-to-all-start.2) | async-done | bytes 811040 | tf_op jit(solution)/shard_map/all_to_all | solution.py:54
  142.7 32.9 %all_to_all.27 = f32[32,1,3072]{2,1,0:T(1,128)S(1)} all-to-all(f32[32,1,3072]{2,1,0:T(1,128)S(1)} %broadcast_in_dim.40), channel_id=1, replica_groups=mesh['row_0'=4,'row_1'=4,'row_2'=2,'col'=16] {'row_2','col'}, dimensions={0} | all-to-all | bytes 786432 | tf_op jit(solution)/shard_map/all_to_all | solution.py:15
  175.9 10.9 %all_to_all.28 = f32[16,1,3072]{2,1,0:T(1,128)S(1)} all-to-all(f32[16,1,3072]{2,1,0:T(1,128)S(1)} %broadcast_in_dim.41), channel_id=1, replica_groups=mesh['row_0'=4,'row_1'=4,'row_2'=2,'col'=16] {'row_0','row_1'}, dimensions={0} | all-to-all | bytes 393216 | tf_op jit(solution)/shard_map/all_to_all | solution.py:15
  188.1 2.9 %cholesky.16 = f32[32,32]{1,0:T(8,128)S(1)} custom-call(f32[32,32]{1,0:T(8,128)S(1)} %fusion.11), custom_call_target="Cholesky" | custom-call | tf_op jit(solution)/shard_map/jit(cholesky)/cholesky | solution.py:161
  192.4 2.4 %custom-call.7 = f32[1,32,32]{1,2,0:T(8,128)S(1)} custom-call(f32[1,32,32]{2,1,0:T(8,128)S(1)} %fusion.9), custom_call_target="InvertDiagBlocksLowerTriangular" | custom-call | tf_op jit(solution)/shard_map/jit(_solve_triangular)/triangular_solve | solution.py:162
  (90 shorter events, 36.9 us)
Async XLA Ops:
  1.6 22.2 %all-to-all-start = ((bf16[32,32,192]{2,1,0:T(8,128)(2,1)}), bf16[32,32,192]{2,1,0:T(8,128)(2,1)S(1)}, u32[]{:S(2)}, u32[]{:S(2)}) async-start(bf16[32,32,192]{2,1,0:T(8,128)(2,1)} %broadcast_in_dim.23), calls=%async_computation | async-start | bytes 1048576 | tf_op jit(solution)/shard_map/all_to_all | solution.py:15
  24.6 41.1 %all-to-all-start.1 = ((bf16[16,192,65]{1,2,0:T(8,128)(2,1)}), bf16[16,192,65]{1,2,0:T(8,128)(2,1)S(1)}, u32[]{:S(2)}, u32[]{:S(2)}) async-start(bf16[16,192,65]{1,2,0:T(8,128)(2,1)} %stack.2), calls=%async_computation.1 | async-start | bytes 1179648 | tf_op jit(solution)/shard_map/all_to_all | solution.py:36
  111.6 10.4 %copy-start = (f32[32,192]{1,0:T(8,128)S(1)}, f32[32,192]{1,0:T(8,128)}, u32[]{:S(2)}) copy-start(f32[32,192]{1,0:T(8,128)} %param.7) | copy-start | bytes 73732
  113.4 28.4 %all-to-all-start.2 = ((f32[32,33,192]{2,1,0:T(8,128)}), f32[32,33,192]{2,1,0:T(8,128)S(1)}, u32[]{:S(2)}, u32[]{:S(2)}) async-start(f32[32,33,192]{2,1,0:T(8,128)} %copy.47), calls=%async_computation.2 | async-start | bytes 2621440 | tf_op jit(solution)/shard_map/all_to_all | solution.py:54
